TPU v7x, 32 devices: a whole 2x2x4 slice. The times are simulated.
32 devices in a mesh: freq: 4 (over z), mic: 8 (over y, x, core).
Axes of the slice: x: 2, y: 2, z: 4, core: 2. Of those that a mesh axis runs over, the one named last changes fastest.
Arguments:
- spectra: float32 [8, 2048, 1024], P('freq', 'mic'), parts along dimension 0, may hold values from -50 to 50
- mic_pos: float32 [3, 2048], replicated, may hold values from -1 to 1
- focus_pts: float32 [3, 1024], replicated, may hold values from -1 to 1
- wavenumber: float32 [4], P('freq'), parts along dimension 0, may hold values from 20 to 120
Outputs:
- csm: float32 [8, 2048, 2048], P('freq', 'mic'), parts along dimension 0
- beam: float32 [4096], P(('freq', 'mic')), parts along dimension 0
There are 4 independent parts, one for each index of `freq`. A program takes and returns all parts, laid end to end along the dimension named above; an argument that names none is the same for every part. Nothing has to cross between parts.
All inputs are finite; a program needn't handle non-finite values.
Results may differ from a plain program's by a relative error of at most 0.0003.
Values sent between devices are 32-bit elements; how exact they have to be, the bound alone decides.
A program may use at most 128 MiB of HBM per device.

v0:
```python
import math

import jax
import jax.numpy as jnp
from jax import lax
from jax.sharding import PartitionSpec as P

standoff_sq = 2.25


def inner(left, right):
    return lax.dot_general(
        left,
        right,
        (((1,), (1,)), ((), ())),
        precision=lax.Precision.HIGHEST,
        preferred_element_type=jnp.float32,
    )


def contract(left, right):
    return lax.dot_general(
        left,
        right,
        (((0,), (0,)), ((), ())),
        precision=lax.Precision.HIGHEST,
        preferred_element_type=jnp.float32,
    )


def cross_block(rows, cols, count):
    real_part = (inner(rows[0], cols[0]) + inner(rows[1], cols[1])) / count
    imag_part = (inner(rows[1], cols[0]) - inner(rows[0], cols[1])) / count
    return jnp.stack([real_part, imag_part])


def steering(mic_pos, focus_pts, wave, count):
    diff = mic_pos[:, :, None] - focus_pts[:, None, :]
    dist = jnp.sqrt(diff[0] * diff[0] + diff[1] * diff[1] + diff[2] * diff[2] + standoff_sq)
    phase = wave * dist
    scale = 1.0 / math.sqrt(count)
    return (jnp.cos(phase) * scale, -jnp.sin(phase) * scale)


def per_device(spectra, mic_pos, focus_pts, wavenumber):
    count = spectra.shape[2]
    all_mics = mic_pos.shape[1]
    all_focus = focus_pts.shape[1]
    n_dev = lax.axis_size("mic")
    me_index = lax.axis_index("mic")
    wave = wavenumber[0]
    own_count = all_focus // n_dev
    own_focus = lax.dynamic_slice_in_dim(focus_pts, me_index * own_count, own_count, 1)
    piece = lax.all_gather(spectra, "mic", axis=1, tiled=True)
    block = cross_block(spectra, piece, count)
    g_real, g_imag = steering(mic_pos, own_focus, wave, all_mics)
    along_real = contract(g_real, piece[0]) + contract(g_imag, piece[1])
    along_imag = contract(g_real, piece[1]) - contract(g_imag, piece[0])
    squares = jnp.sum(piece[0] * piece[0] + piece[1] * piece[1])
    csm, along_real, along_imag, squares = (block, along_real, along_imag, squares)
    power = jnp.sum(along_real * along_real + along_imag * along_imag, axis=1) / count
    beam = power - squares / count / all_mics
    return (csm, beam)


def solution(mesh):
    in_specs = (P("freq", "mic", None), P(), P(), P("freq"))
    out_specs = (P("freq", "mic", None), P(("freq", "mic")))
    return jax.shard_map(
        per_device, mesh=mesh, in_specs=in_specs, out_specs=out_specs, check_vma=False
    )
```

profile of v0, /device:TPU:0, one launch (start us, length us, event | category | flops | bytes accessed | tf_op | source)
XLA Modules:
  0.0 190.7 jit_solution(7960682727829128553)
XLA Ops:
  7.2 0.0 copy-start
  7.2 0.0 all-gather.2.cloned.1.call-start
  7.2 0.7 all-gather.2.cloned.1.call-update
  8.6 0.0 copy-done
  8.6 1.6 broadcast_subtract_fusion
  10.2 0.5 fusion.23
  10.7 91.8 %all-gather.2.cloned.1.call-done = f32[2,2048,1024]{2,1,0:T(8,128)} async-done(((f32[2,256,1024]{2,1,0:T(8,128)}), f32[2,2048,1024]{2,1,0:T(8,128)}) %all-gather.2.cloned.1.call-update) | async-done | bytes 16777232 | tf_op jit(solution)/shard_map/all_gather | solution.py:54
  102.5 7.7 %add_reduce_fusion = f32[]{:T(128)} fusion(f32[2,2048,1024]{2,1,0:T(8,128)} %all-gather.2.cloned.1.call-done), kind=kLoop, calls=%fused_computation.2 | loop fusion | flops 8388607 | bytes 16777220 | tf_op jit(solution)/shard_map/reduce_sum | solution.py:59
  110.9 0.0 copy-start.1
  110.9 11.6 %fusion.1 = f32[128,1024]{1,0:T(8,128)S(1)} fusion(f32[2,2048,1024]{2,1,0:T(8,128)} %all-gather.2.cloned.1.call-done, f32[1,2048,128]{2,1,0:T(8,128)S(1)} %fusion.23), kind=kOutput, calls=%fused_computation.4 | convolution fusion | flops 3221487616 | bytes 9961472 | tf_op jit(solution)/shard_map/dot_general | solution.py:22
  122.5 11.8 %fusion = f32[128,1024]{1,0:T(8,128)S(1)} fusion(f32[2,2048,1024]{2,1,0:T(8,128)} %all-gather.2.cloned.1.call-done, f32[1,2048,128]{2,1,0:T(8,128)S(1)} %fusion.23), kind=kOutput, calls=%fused_computation.3 | convolution fusion | flops 3221749760 | bytes 9961472 | tf_op jit(solution)/shard_map/dot_general | solution.py:22
  134.3 0.0 copy-done.1
  134.3 0.0 copy-start.2
  134.3 8.3 %fusion.15 = f32[128,1024]{1,0:T(8,128)S(1)} fusion(f32[128,1024]{1,0:T(8,128)S(1)} %fusion.1, f32[2,2048,1024]{2,1,0:T(8,128)S(1)} %copy-done.1, f32[1,2048,128]{2,1,0:T(8,128)S(1)} %fusion.23), kind=kOutput, calls=%fused_computation.20 | convolution fusion | flops 3222011904 | bytes 10485760 | tf_op jit(solution)/shard_map/dot_general | solution.py:22
  142.6 8.1 %fusion.19 = f32[128]{0:T(128)S(1)} fusion(f32[128,1024]{1,0:T(8,128)S(1)} %fusion.15, f32[128,1024]{1,0:T(8,128)S(1)} %fusion, f32[2,2048,1024]{2,1,0:T(8,128)S(1)} %copy-done.1, f32[1,2048,128]{2,1,0:T(8,128)S(1)} %fusion.23), kind=kOutput, calls=%fused_computation.24 | convolution fusion | flops 3222011904 | bytes 10486272 | tf_op jit(solution)/shard_map/dot_general | solution.py:22
  150.8 0.5 multiply_subtract_fusion
  151.3 0.0 copy-done.2
  151.3 7.5 %fusion.3 = f32[256,2048]{1,0:T(8,128)S(1)} fusion(f32[2,2048,1024]{2,1,0:T(8,128)S(1)} %copy-done.1, f32[2,256,1024]{2,1,0:T(8,128)S(1)} %copy-done.2), kind=kOutput, calls=%fused_computation.6 | convolution fusion | flops 6442450944 | bytes 11534336 | tf_op jit(solution)/shard_map/dot_general | solution.py:12
  158.8 7.3 %fusion.2 = f32[256,2048]{1,0:T(8,128)S(1)} fusion(f32[2,2048,1024]{2,1,0:T(8,128)S(1)} %copy-done.1, f32[2,256,1024]{2,1,0:T(8,128)S(1)} %copy-done.2), kind=kOutput, calls=%fused_computation.5 | convolution fusion | flops 6442450944 | bytes 11534336 | tf_op jit(solution)/shard_map/dot_general | solution.py:12
  166.1 7.6 %fusion.10 = f32[1,256,2048]{2,1,0:T(8,128)S(1)} fusion(f32[256,2048]{1,0:T(8,128)S(1)} %fusion.3, f32[2,2048,1024]{2,1,0:T(8,128)S(1)} %copy-done.1, f32[2,256,1024]{2,1,0:T(8,128)S(1)} %copy-done.2), kind=kOutput, calls=%fused_computation.14 | convolution fusion | flops 6443499520 | bytes 13631488 | tf_op jit(solution)/shard_map/dot_general | solution.py:12
  173.8 7.3 %fusion.13 = f32[1,256,2048]{2,1,0:T(8,128)S(1)} fusion(f32[256,2048]{1,0:T(8,128)S(1)} %fusion.2, f32[2,2048,1024]{2,1,0:T(8,128)S(1)} %copy-done.1, f32[2,256,1024]{2,1,0:T(8,128)S(1)} %copy-done.2), kind=kOutput, calls=%fused_computation.17 | convolution fusion | flops 6443499520 | bytes 13631488 | tf_op jit(solution)/shard_map/dot_general | solution.py:12
  181.1 2.3 %pad_maximum_fusion = f32[2,256,2048]{2,1,0:T(8,128)} fusion(f32[1,256,2048]{2,1,0:T(8,128)S(1)} %fusion.13, f32[1,256,2048]{2,1,0:T(8,128)S(1)} %fusion.10), kind=kLoop, calls=%fused_computation.11 | loop fusion | flops 1048576 | bytes 8388608 | tf_op jit(solution)/shard_map/stack | solution.py:34
  (1 shorter events, 0.0 us)
Async XLA Ops:
  7.2 1.4 copy-start
  7.2 95.3 %all-gather.2.cloned.1.call-start = ((), (), s32[]{:S(2)}) async-start(), calls=%async_computation | async-start | bytes 18874368 | tf_op jit(solution)/shard_map/all_gather | solution.py:54
  110.9 23.4 %copy-start.1 = (f32[2,2048,1024]{2,1,0:T(8,128)S(1)}, f32[2,2048,1024]{2,1,0:T(8,128)}, u32[]{:S(2)}) copy-start(f32[2,2048,1024]{2,1,0:T(8,128)} %all-gather.2.cloned.1.call-done) | copy-start | bytes 50331652
  134.3 17.0 %copy-start.2 = (f32[2,256,1024]{2,1,0:T(8,128)S(1)}, f32[2,256,1024]{2,1,0:T(8,128)}, u32[]{:S(2)}) copy-start(f32[2,256,1024]{2,1,0:T(8,128)} %param.4) | copy-start | bytes 6291460
Sparse Core Ops, SparseCore 0:
  9.9 92.5 all-gather.1
where the time goes:
time: 193 us; the launch traced here: 191 us
  waiting for transfers between devices  92.5 us (48%)
  matrix products  69.6 us (36%)
  between operations  15.9 us (8%)
  other arithmetic  12.7 us (7%)
    all_gather x1, waiting for transfers between devices, per_device(): piece = lax.all_gather(spectra, 'mic', axis=1, tiled=True)  91.8 us
    dot_general x4, matrix products, contract(): lax.dot_general(left, right, (((0,), (0,)), ((), ())), precision=lax.Prec...  39.8 us
    dot_general x4, matrix products, inner(): lax.dot_general(left, right, (((1,), (1,)), ((), ())), precision=lax.Prec...  29.8 us
    reduce_sum x1, other arithmetic, per_device(): squares = jnp.sum(piece[0] * piece[0] + piece[1] * piece[1])  7.74 us
  transfers between devices with their start and end apart: 1, of which 1 were waited for; matrix products, arithmetic and copies ran while one was open for 1% of the time, Pallas kernels for 0%

commit v1 on v0

--- a/solution.py
+++ b/solution.py
@@ -1,11 +1,18 @@
+import functools
 import math
 
 import jax
 import jax.numpy as jnp
 from jax import lax
+from jax.experimental import pallas as pl
+from jax.experimental.pallas import tpu as pltpu
 from jax.sharding import PartitionSpec as P
 
 standoff_sq = 2.25
+MESH = pl.DeviceIdType.MESH
+
+SIN_COEF = (3.141592640144165, -5.167710084047848, 2.550077528428822, -0.598291299770303, 0.07765766117753167)
+COS_COEF = (0.9999999532943689, -4.934792832496617, 4.058411371007551, -1.331876617475819, 0.21968961468319229)
 
 
 def inner(left, right):
@@ -13,7 +20,7 @@
         left,
         right,
         (((1,), (1,)), ((), ())),
-        precision=lax.Precision.HIGHEST,
+        precision=lax.Precision.HIGH,
         preferred_element_type=jnp.float32,
     )
 
@@ -23,7 +30,7 @@
         left,
         right,
         (((0,), (0,)), ((), ())),
-        precision=lax.Precision.HIGHEST,
+        precision=lax.Precision.HIGH,
         preferred_element_type=jnp.float32,
     )
 
@@ -42,7 +49,7 @@
     return (jnp.cos(phase) * scale, -jnp.sin(phase) * scale)
 
 
-def per_device(spectra, mic_pos, focus_pts, wavenumber):
+def general(spectra, mic_pos, focus_pts, wavenumber):
     count = spectra.shape[2]
     all_mics = mic_pos.shape[1]
     all_focus = focus_pts.shape[1]
@@ -57,13 +64,422 @@
     along_real = contract(g_real, piece[0]) + contract(g_imag, piece[1])
     along_imag = contract(g_real, piece[1]) - contract(g_imag, piece[0])
     squares = jnp.sum(piece[0] * piece[0] + piece[1] * piece[1])
-    csm, along_real, along_imag, squares = (block, along_real, along_imag, squares)
     power = jnp.sum(along_real * along_real + along_imag * along_imag, axis=1) / count
     beam = power - squares / count / all_mics
-    return (csm, beam)
+    return (block, beam)
+
+
+HALF = 128
+BLOCK = 256
+
+
+def dot_nt(left, right):
+    return lax.dot_general(left, right, (((1,), (1,)), ((), ())), preferred_element_type=jnp.float32)
+
+
+def dot_nn(left, right):
+    return lax.dot_general(left, right, (((1,), (0,)), ((), ())), preferred_element_type=jnp.float32)
+
+
+def dot3(dot, left, right):
+    return dot(left[0], right[0]) + (dot(left[0], right[1]) + dot(left[1], right[0]))
+
+
+def split(value):
+    high = value.astype(jnp.bfloat16)
+    low = (value - high.astype(jnp.float32)).astype(jnp.bfloat16)
+    return high, low
+
+
+def horner(coef, z):
+    out = jnp.full_like(z, coef[-1])
+    for c in coef[-2::-1]:
+        out = out * z + c
+    return out
+
+
+def kernel(
+    x_ref, mic_ref, foc_ref, wave_ref, c_ref, beam_ref,
+    own, recv, xh, xl, gh, gl, cst, chl, dbuf, dhb, pacc, ptx, prx,
+    loc_sem, out_sem, ss, rs, fs, fr, ds, dr, bs, br,
+):
+    count = x_ref.shape[2]
+    all_mics = mic_ref.shape[1]
+    all_focus = foc_ref.shape[1]
+    me = lax.axis_index("mic")
+    y, x, h = me // 4, (me // 2) % 2, me % 2
+
+    def index(yy, xx, hh):
+        return yy * 4 + xx * 2 + hh
+
+    sib = index(y, x, 1 - h)
+    xd, xo = index(y, 1 - x, h), index(y, 1 - x, 1 - h)
+    yd, yo = index(1 - y, x, (h + y) % 2), index(1 - y, x, (h + y + 1) % 2)
+    yt = index(1 - y, x, (h + 1 - y) % 2)
+
+    barrier = pltpu.get_barrier_semaphore()
+    for j in range(1, 8):
+        pl.semaphore_signal(barrier, inc=1, device_id={"mic": (me + j) % 8}, device_id_type=MESH)
+    pl.semaphore_wait(barrier, 7)
+
+    def half(t):
+        return pl.ds(pl.multiple_of(t * HALF, HALF), HALF)
+
+    def main_copy(t, which):
+        return pltpu.make_async_remote_copy(
+            src_ref=x_ref.at[:, half(t), :],
+            dst_ref=recv.at[1 + which, :, half(t), :],
+            send_sem=ss.at[1 + 2 * t + which],
+            recv_sem=rs.at[1 + 2 * t + which],
+            device_id={"mic": yt if which else xd},
+            device_id_type=MESH,
+        )
+
+    def forward(t, which):
+        return pltpu.make_async_remote_copy(
+            src_ref=recv.at[1 + which, :, half(t), :],
+            dst_ref=recv.at[3 + which, :, half(t), :],
+            send_sem=fs.at[2 * t + which],
+            recv_sem=fr.at[2 * t + which],
+            device_id={"mic": sib},
+            device_id_type=MESH,
+        )
+
+    sib_copy = pltpu.make_async_remote_copy(
+        src_ref=x_ref,
+        dst_ref=recv.at[0],
+        send_sem=ss.at[0],
+        recv_sem=rs.at[0],
+        device_id={"mic": sib},
+        device_id_type=MESH,
+    )
+
+    def cols(dev, t):
+        return pl.ds(pl.multiple_of(dev * BLOCK + t * HALF, HALF), HALF)
+
+    def piece_copy(p, role):
+        a, b = p // 2, p % 2
+        if role == 0:
+            src, rows, to = dbuf.at[p], half(a), xd
+            where = cols(yd, b)
+        else:
+            src, rows, to = dhb.at[p], half(b), yd
+            where = cols(xd, a)
+        return pltpu.make_async_remote_copy(
+            src_ref=src,
+            dst_ref=c_ref.at[:, rows, where],
+            send_sem=ds.at[2 * p + role],
+            recv_sem=dr.at[2 * p + role],
+            device_id={"mic": to},
+            device_id_type=MESH,
+        )
+
+    def out_copy(v, dev, t, hf):
+        return pltpu.make_async_copy(
+            cst.at[v, :, :, hf * HALF : (hf + 1) * HALF],
+            c_ref.at[:, :, cols(dev, t)],
+            out_sem.at[2 * v + hf],
+        )
+
+    for t in range(2):
+        main_copy(t, 0).start()
+        main_copy(t, 1).start()
+        if t == 0:
+            sib_copy.start()
+    own_copy = pltpu.make_async_copy(x_ref, own, loc_sem)
+    own_copy.start()
+
+    pacc[...] = jnp.zeros_like(pacc)
+
+    turns = wave_ref[0] * (0.5 / math.pi)
+    owners = [(me, me), (sib, sib), (xd, yd), (xo, yo), (xd, yd), (xo, yo)]
+
+    def steer_half(v, hf):
+        dev = owners[v][hf]
+        t = hf if v < 2 else (v - 2) // 2
+        at = cols(dev, t)
+        mic = [
+            jnp.transpose(jnp.broadcast_to(mic_ref[c : c + 1, at], (HALF, HALF))) for c in range(3)
+        ]
+
+        def tile(n, carry):
+            lanes = pl.ds(pl.multiple_of(n * HALF, HALF), HALF)
+            total = None
+            for c in range(3):
+                d = mic[c] - foc_ref[c : c + 1, lanes]
+                total = d * d if total is None else total + d * d
+            turn = turns * jnp.sqrt(total + standoff_sq)
+            f = turn - jnp.round(turn)
+            z = f * f
+            s = f * horner(SIN_COEF, z)
+            c = horner(COS_COEF, z)
+            both = (1.0 - 2.0 * s * s, -2.0 * s * c)
+            for k in range(2):
+                high, low = split(both[k])
+                gh[v, k, hf * HALF : (hf + 1) * HALF, lanes] = high
+                gl[v, k, hf * HALF : (hf + 1) * HALF, lanes] = low
+            return carry
+
+        lax.fori_loop(0, all_focus // HALF, tile, 0)
+
+    def split_rows(load, v, row, rows):
+        step = 32
+
+        def body(i, carry):
+            for k in range(2):
+                high, low = split(load(k, i * step, step))
+                at = pl.ds(pl.multiple_of(row + i * step, step), step)
+                xh[v, k, at, :] = high
+                xl[v, k, at, :] = low
+            return carry
+
+        lax.fori_loop(0, rows // step, body, 0)
+
+    def spectra_of(v, k, rows):
+        return xh[v, k, rows, :], xl[v, k, rows, :]
+
+    def cross(v_left, rows_left, v_right, rows_right):
+        left = [spectra_of(v_left, k, rows_left) for k in range(2)]
+        right = [spectra_of(v_right, k, rows_right) for k in range(2)]
+        real = dot3(dot_nt, left[0], right[0]) + dot3(dot_nt, left[1], right[1])
+        imag = dot3(dot_nt, left[1], right[0]) - dot3(dot_nt, left[0], right[1])
+        return real * (1.0 / count), imag * (1.0 / count)
+
+    whole = slice(0, BLOCK)
+    first, second = slice(0, HALF), slice(HALF, BLOCK)
+
+    def csm_block(v):
+        real, imag = cross(0, whole, v, whole)
+        cst[v, 0] = real
+        cst[v, 1] = imag
+
+    def power(m, left, right, weight):
+        width = 256
+
+        def tile(n, carry):
+            lanes = pl.ds(pl.multiple_of(n * width, width), width)
+            c = [(chl[0, k, :m, :], chl[1, k, :m, :]) for k in range(2)]
+            g = [right(k, lanes) for k in range(2)]
+            zr = dot3(dot_nn, c[0], g[0]) - dot3(dot_nn, c[1], g[1])
+            zi = dot3(dot_nn, c[0], g[1]) + dot3(dot_nn, c[1], g[0])
+            lr, li = left(0, lanes), left(1, lanes)
+            p = lr * zr + li * zi
+            p = jnp.sum(p.reshape(m // 8, 8, width), axis=0)
+            pacc[:, lanes] += weight * p
+            return carry
+
+        lax.fori_loop(0, all_focus // width, tile, 0)
+
+    def beam_block(v, drop_diagonal):
+        for k in range(2):
+            value = cst[v, k]
+            if drop_diagonal is not None and k == 0:
+                row = lax.broadcasted_iota(jnp.int32, (BLOCK, BLOCK), 0)
+                col = lax.broadcasted_iota(jnp.int32, (BLOCK, BLOCK), 1)
+                value = jnp.where((row == col) & drop_diagonal, 0.0, value)
+            high, low = split(value)
+            chl[0, k] = high
+            chl[1, k] = low
+
+        def left(k, lanes):
+            return gh[0, k, :, lanes].astype(jnp.float32) + gl[0, k, :, lanes].astype(jnp.float32)
+
+        def right(k, lanes):
+            return gh[v, k, :, lanes], gl[v, k, :, lanes]
+
+        power(BLOCK, left, right, 1.0)
+
+    for v in range(2):
+        for hf in range(2):
+            steer_half(v, hf)
+    own_copy.wait()
+    split_rows(lambda k, r, n: own[k, pl.ds(pl.multiple_of(r, n), n), :], 0, 0, BLOCK)
+    sib_copy.wait_recv()
+    split_rows(lambda k, r, n: recv[0, k, pl.ds(pl.multiple_of(r, n), n), :], 1, 0, BLOCK)
+
+    def near(v, carry):
+        csm_block(v)
+        beam_block(v, v == 0)
+        return carry
+
+    lax.fori_loop(0, 2, near, 0)
+    for hf in range(2):
+        out_copy(0, me, hf, hf).start()
+        out_copy(1, sib, hf, hf).start()
+    for v in range(2, 6):
+        for hf in range(2):
+            steer_half(v, hf)
+
+    def phase(t, carry):
+        def rows_of(slot):
+            def load(k, r, n):
+                return recv[slot, k, pl.ds(pl.multiple_of(t * HALF + r, n), n), :]
+            return load
+
+        for which in range(2):
+            main_copy(t, which).wait_recv()
+            forward(t, which).start()
+        split_rows(rows_of(1), 2 + 2 * t, 0, HALF)
+        split_rows(rows_of(2), 2 + 2 * t, HALF, HALF)
+
+        def piece(p, inner_carry):
+            real, imag = cross(2 + 2 * (p // 2), first, 2 + 2 * (p % 2), second)
+            dbuf[p, 0] = real
+            dbuf[p, 1] = imag
+            piece_copy(p, 0).start()
+            dhb[p, 0] = jnp.transpose(real)
+            dhb[p, 1] = -jnp.transpose(imag)
+            piece_copy(p, 1).start()
+            return inner_carry
+
+        lax.fori_loop(t, 1 + 3 * t, piece, 0)
+
+        def far(o, inner_carry):
+            v = 2 + 2 * t + o
+            csm_block(v)
+            beam_block(v, None)
+            return inner_carry
+
+        for which in range(2):
+            forward(t, which).wait_recv()
+        split_rows(rows_of(3), 3 + 2 * t, 0, HALF)
+        split_rows(rows_of(4), 3 + 2 * t, HALF, HALF)
+        lax.fori_loop(0, 2, far, 0)
+        out_copy(2 + 2 * t, xd, t, 0).start()
+        out_copy(2 + 2 * t, yd, t, 1).start()
+        out_copy(3 + 2 * t, xo, t, 0).start()
+        out_copy(3 + 2 * t, yo, t, 1).start()
+        return carry
+
+    lax.fori_loop(0, 2, phase, 0)
+
+    def mirrored(a, carry):
+        for k in range(2):
+            for b in range(2):
+                high, low = split(dbuf[2 * a + b, k])
+                chl[0, k, :HALF, b * HALF : (b + 1) * HALF] = high
+                chl[1, k, :HALF, b * HALF : (b + 1) * HALF] = low
+
+        def left(k, lanes):
+            v = 2 + 2 * a
+            return gh[v, k, first, lanes].astype(jnp.float32) + gl[v, k, first, lanes].astype(jnp.float32)
+
+        def right(k, lanes):
+            return tuple(
+                jnp.concatenate([g[2, k, second, lanes], g[4, k, second, lanes]], axis=0)
+                for g in (gh, gl)
+            )
+
+        power(HALF, left, right, 2.0)
+        return carry
+
+    lax.fori_loop(0, 2, mirrored, 0)
+
+    for j in range(8):
+        ptx[j] = jnp.sum(pacc[:, j * HALF : (j + 1) * HALF], axis=0, keepdims=True) * (1.0 / all_mics)
+
+    def beam_copy(j):
+        to = (me + j) % 8
+        return pltpu.make_async_remote_copy(
+            src_ref=ptx.at[to],
+            dst_ref=prx.at[j],
+            send_sem=bs.at[j],
+            recv_sem=br.at[j],
+            device_id={"mic": to},
+            device_id_type=MESH,
+        )
+
+    for j in range(1, 8):
+        beam_copy(j).start()
+    total = ptx[me]
+    for j in range(1, 8):
+        beam_copy(j).wait_recv()
+        total = total + prx[j]
+    beam_ref[...] = total
+
+    for j in range(1, 8):
+        beam_copy(j).wait_send()
+    sib_copy.wait_send()
+    for t in range(2):
+        for which in range(2):
+            main_copy(t, which).wait_send()
+            forward(t, which).wait_send()
+    for hf in range(2):
+        out_copy(0, me, hf, hf).wait()
+        out_copy(1, sib, hf, hf).wait()
+    for t in range(2):
+        out_copy(2 + 2 * t, xd, t, 0).wait()
+        out_copy(2 + 2 * t, yd, t, 1).wait()
+        out_copy(3 + 2 * t, xo, t, 0).wait()
+        out_copy(3 + 2 * t, yo, t, 1).wait()
+    for p in range(4):
+        for role in range(2):
+            piece_copy(p, role).wait_send()
+            piece_copy(p, role).wait_recv()
+
+
+def exchange(spectra, mic_pos, focus_pts, wavenumber):
+    rows, count = spectra.shape[1:]
+    all_mics = mic_pos.shape[1]
+    all_focus = focus_pts.shape[1]
+    f32, bf16 = jnp.float32, jnp.bfloat16
+    dma = pltpu.SemaphoreType.DMA
+    csm, beam = pl.pallas_call(
+        kernel,
+        out_shape=(
+            jax.ShapeDtypeStruct((2, rows, all_mics), f32),
+            jax.ShapeDtypeStruct((1, all_focus // 8), f32),
+        ),
+        in_specs=[
+            pl.BlockSpec(memory_space=pl.ANY),
+            pl.BlockSpec(memory_space=pltpu.VMEM),
+            pl.BlockSpec(memory_space=pltpu.VMEM),
+            pl.BlockSpec(memory_space=pltpu.SMEM),
+        ],
+        out_specs=(pl.BlockSpec(memory_space=pl.ANY), pl.BlockSpec(memory_space=pltpu.VMEM)),
+        scratch_shapes=[
+            pltpu.VMEM((2, rows, count), f32),
+            pltpu.VMEM((5, 2, rows, count), f32),
+            pltpu.VMEM((6, 2, rows, count), bf16),
+            pltpu.VMEM((6, 2, rows, count), bf16),
+            pltpu.VMEM((6, 2, rows, all_focus), bf16),
+            pltpu.VMEM((6, 2, rows, all_focus), bf16),
+            pltpu.VMEM((6, 2, rows, rows), f32),
+            pltpu.VMEM((2, 2, rows, rows), bf16),
+            pltpu.VMEM((4, 2, HALF, HALF), f32),
+            pltpu.VMEM((4, 2, HALF, HALF), f32),
+            pltpu.VMEM((8, all_focus), f32),
+            pltpu.VMEM((8, 1, HALF), f32),
+            pltpu.VMEM((8, 1, HALF), f32),
+            dma(()),
+            dma((12,)),
+            dma((5,)),
+            dma((5,)),
+            dma((4,)),
+            dma((4,)),
+            dma((8,)),
+            dma((8,)),
+            dma((8,)),
+            dma((8,)),
+        ],
+        compiler_params=pltpu.CompilerParams(
+            collective_id=0, has_side_effects=True, vmem_limit_bytes=58 * 1024 * 1024
+        ),
+    )(spectra, mic_pos, focus_pts, wavenumber)
+    return csm, beam.reshape(all_focus // 8)
 
 
 def solution(mesh):
+    def per_device(spectra, mic_pos, focus_pts, wavenumber):
+        fits = (
+            mesh.shape["mic"] == 8
+            and spectra.shape[1] == BLOCK
+            and spectra.shape[2] % HALF == 0
+            and focus_pts.shape[1] == 8 * HALF
+        )
+        body = exchange if fits else general
+        return body(spectra, mic_pos, focus_pts, wavenumber)
+
     in_specs = (P("freq", "mic", None), P(), P(), P("freq"))
     out_specs = (P("freq", "mic", None), P(("freq", "mic")))
     return jax.shard_map(

time: 193 us -> 78.4 us (0.41); the launches traced: 191 us -> 78.1 us
  waiting for transfers between devices: 92.5 us -> 0 us
  Pallas kernels: 0 us -> 71.6 us
  matrix products: 69.6 us -> 0 us
  between operations: 15.9 us -> 1.29 us
  other arithmetic: 12.7 us -> 0 us
  local copies, waits for them, and re-layouts: 0.03 us -> 5.21 us
    all_gather x1 -> x0, waiting for transfers between devices: 91.8 us -> none  [per_device(): piece = lax.all_gather(spectra, 'mic', axis=1, tiled=True)]
    pallas_call x0 -> x1, Pallas kernels: none -> 71.6 us  [exchange(): pl.pallas_call(kernel, out_shape=(jax.ShapeDtypeStruct((2, rows, all_mics...]
    dot_general x8 -> x0, matrix products: 69.6 us -> none  [the longest x4 39.8 us: contract(): lax.dot_general(left, right, (((0,), (0,)), ((), ())), precision=lax.Prec...]
    reduce_sum x1 -> x0, other arithmetic: 7.74 us -> none  [per_device(): squares = jnp.sum(piece[0] * piece[0] + piece[1] * piece[1])]
    unnamed x6 -> x4, local copies, waits for them, and re-layouts: 0.02 us -> 5.21 us
    another operation x1 -> x0, other arithmetic: 2.28 us -> none  [cross_block(): return jnp.stack([real_part, imag_part])]
    sub x2 -> x0, other arithmetic: 2.16 us -> none  [the longest x1 1.63 us: steering(): diff = mic_pos[:, :, None] - focus_pts[:, None, :]]
  transfers between devices with their start and end apart: 1 -> 0, of which waited for: 1 -> 0; matrix products, arithmetic and copies ran while one was open for 1% -> 0% of each run, Pallas kernels for 0% -> 0%
where the time goes in v1:
time: 78.4 us; the launch traced here: 78.1 us
  Pallas kernels  71.6 us (91%)
  local copies, waits for them, and re-layouts  5.21 us (7%)
  between operations  1.29 us (2%)
    pallas_call x1, Pallas kernels, exchange(): pl.pallas_call(kernel, out_shape=(jax.ShapeDtypeStruct((2, rows, all_mics...  71.6 us
    unnamed x4, local copies, waits for them, and re-layouts  5.21 us

profile of v1, /device:TPU:0, one launch (start us, length us, event | category | flops | bytes accessed | tf_op | source)
XLA Modules:
  0.0 78.1 jit_solution(7296524658888764646)
XLA Ops:
  1.3 71.6 %shard_map.59 = (f32[2,256,2048]{2,1,0:T(8,128)}, f32[1,128]{1,0:T(1,128)}) custom-call(f32[2,256,1024]{2,1,0:T(8,128)} %x_ref.1, f32[3,2048]{1,0:T(4,128)} %mic_ref.1, f32[3,1024]{1,0:T(4,128)} %foc_ref.1, f32[1]{0:T(128)S(6)} %copy.8.wave_ref), custom_call_target="tpu_custom_call" | custom-call | tf_op jit(solution)/shard_map/pallas_call | solution.py:427
  72.9 0.0 copy-start
  72.9 4.7 %copy.9 = f32[2,256,2048]{2,1,0:T(8,128)} copy(f32[2,256,2048]{2,1,0:T(8,128)} %get-tuple-element.8) | data formatting | bytes 8388608
  77.6 0.0 copy-done
  77.6 0.5 copy.10
Async XLA Ops:
  72.9 4.7 %copy-start = (f32[1,128]{1,0:T(1,128)S(1)}, f32[1,128]{1,0:T(1,128)}, u32[]{:S(2)}) copy-start(f32[1,128]{1,0:T(1,128)} %get-tuple-element.5) | copy-start | bytes 1540

commit v2 on v1

--- a/solution.py
+++ b/solution.py
@@ -270,24 +270,28 @@
 
         lax.fori_loop(0, all_focus // width, tile, 0)
 
-    def beam_block(v, drop_diagonal):
+    def beam_block(v, drop_diagonal, row=0, late_weight=1.0):
+        m = BLOCK - row
         for k in range(2):
-            value = cst[v, k]
+            value = cst[v, k, row:, :]
             if drop_diagonal is not None and k == 0:
-                row = lax.broadcasted_iota(jnp.int32, (BLOCK, BLOCK), 0)
-                col = lax.broadcasted_iota(jnp.int32, (BLOCK, BLOCK), 1)
-                value = jnp.where((row == col) & drop_diagonal, 0.0, value)
+                r = lax.broadcasted_iota(jnp.int32, (BLOCK, BLOCK), 0)
+                c = lax.broadcasted_iota(jnp.int32, (BLOCK, BLOCK), 1)
+                value = jnp.where((r == c) & drop_diagonal, 0.0, value)
             high, low = split(value)
-            chl[0, k] = high
-            chl[1, k] = low
+            chl[0, k, :m, :] = high
+            chl[1, k, :m, :] = low
 
         def left(k, lanes):
-            return gh[0, k, :, lanes].astype(jnp.float32) + gl[0, k, :, lanes].astype(jnp.float32)
+            value = gh[0, k, row:, lanes].astype(jnp.float32) + gl[0, k, row:, lanes].astype(jnp.float32)
+            if late_weight == 1.0:
+                return value
+            return jnp.concatenate([value[:HALF], late_weight * value[HALF:]], axis=0)
 
         def right(k, lanes):
             return gh[v, k, :, lanes], gl[v, k, :, lanes]
 
-        power(BLOCK, left, right, 1.0)
+        power(m, left, right, 1.0)
 
     for v in range(2):
         for hf in range(2):
@@ -310,19 +314,43 @@
         for hf in range(2):
             steer_half(v, hf)
 
-    def phase(t, carry):
+    def mirrored(a, carry):
+        for k in range(2):
+            for b in range(2):
+                high, low = split(dbuf[2 * a + b, k])
+                chl[0, k, :HALF, b * HALF : (b + 1) * HALF] = high
+                chl[1, k, :HALF, b * HALF : (b + 1) * HALF] = low
+
+        def left(k, lanes):
+            v = 2 + 2 * a
+            return gh[v, k, first, lanes].astype(jnp.float32) + gl[v, k, first, lanes].astype(jnp.float32)
+
+        def right(k, lanes):
+            return tuple(
+                jnp.concatenate([g[2, k, second, lanes], g[4, k, second, lanes]], axis=0)
+                for g in (gh, gl)
+            )
+
+        power(HALF, left, right, 2.0)
+        return carry
+
+
+    for t in range(2):
         def rows_of(slot):
             def load(k, r, n):
                 return recv[slot, k, pl.ds(pl.multiple_of(t * HALF + r, n), n), :]
             return load
 
-        for which in range(2):
-            main_copy(t, which).wait_recv()
-            forward(t, which).start()
-        split_rows(rows_of(1), 2 + 2 * t, 0, HALF)
-        split_rows(rows_of(2), 2 + 2 * t, HALF, HALF)
-
-        def piece(p, inner_carry):
+        def far(v, x_dev, y_dev):
+            csm_block(v)
+            out_copy(v, x_dev, t, 0).start()
+            out_copy(v, y_dev, t, 1).start()
+            if t == 0:
+                beam_block(v, None, 0, 2.0)
+            else:
+                beam_block(v, None, HALF)
+
+        def piece(p, carry):
             real, imag = cross(2 + 2 * (p // 2), first, 2 + 2 * (p % 2), second)
             dbuf[p, 0] = real
             dbuf[p, 1] = imag
@@ -330,48 +358,20 @@
             dhb[p, 0] = jnp.transpose(real)
             dhb[p, 1] = -jnp.transpose(imag)
             piece_copy(p, 1).start()
-            return inner_carry
-
+            return carry
+
+        for which in range(2):
+            main_copy(t, which).wait_recv()
+            forward(t, which).start()
+        split_rows(rows_of(1), 2 + 2 * t, 0, HALF)
+        split_rows(rows_of(2), 2 + 2 * t, HALF, HALF)
         lax.fori_loop(t, 1 + 3 * t, piece, 0)
-
-        def far(o, inner_carry):
-            v = 2 + 2 * t + o
-            csm_block(v)
-            beam_block(v, None)
-            return inner_carry
-
+        far(2 + 2 * t, xd, yd)
         for which in range(2):
             forward(t, which).wait_recv()
         split_rows(rows_of(3), 3 + 2 * t, 0, HALF)
         split_rows(rows_of(4), 3 + 2 * t, HALF, HALF)
-        lax.fori_loop(0, 2, far, 0)
-        out_copy(2 + 2 * t, xd, t, 0).start()
-        out_copy(2 + 2 * t, yd, t, 1).start()
-        out_copy(3 + 2 * t, xo, t, 0).start()
-        out_copy(3 + 2 * t, yo, t, 1).start()
-        return carry
-
-    lax.fori_loop(0, 2, phase, 0)
-
-    def mirrored(a, carry):
-        for k in range(2):
-            for b in range(2):
-                high, low = split(dbuf[2 * a + b, k])
-                chl[0, k, :HALF, b * HALF : (b + 1) * HALF] = high
-                chl[1, k, :HALF, b * HALF : (b + 1) * HALF] = low
-
-        def left(k, lanes):
-            v = 2 + 2 * a
-            return gh[v, k, first, lanes].astype(jnp.float32) + gl[v, k, first, lanes].astype(jnp.float32)
-
-        def right(k, lanes):
-            return tuple(
-                jnp.concatenate([g[2, k, second, lanes], g[4, k, second, lanes]], axis=0)
-                for g in (gh, gl)
-            )
-
-        power(HALF, left, right, 2.0)
-        return carry
+        far(3 + 2 * t, xo, yo)
 
     lax.fori_loop(0, 2, mirrored, 0)
 
@@ -427,7 +427,7 @@
     csm, beam = pl.pallas_call(
         kernel,
         out_shape=(
-            jax.ShapeDtypeStruct((2, rows, all_mics), f32),
+            pltpu.VMEM((2, rows, all_mics), f32),
             jax.ShapeDtypeStruct((1, all_focus // 8), f32),
         ),
         in_specs=[
@@ -436,7 +436,7 @@
             pl.BlockSpec(memory_space=pltpu.VMEM),
             pl.BlockSpec(memory_space=pltpu.SMEM),
         ],
-        out_specs=(pl.BlockSpec(memory_space=pl.ANY), pl.BlockSpec(memory_space=pltpu.VMEM)),
+        out_specs=(pl.BlockSpec(memory_space=pltpu.VMEM), pl.BlockSpec(memory_space=pltpu.VMEM)),
         scratch_shapes=[
             pltpu.VMEM((2, rows, count), f32),
             pltpu.VMEM((5, 2, rows, count), f32),
@@ -463,7 +463,7 @@
             dma((8,)),
         ],
         compiler_params=pltpu.CompilerParams(
-            collective_id=0, has_side_effects=True, vmem_limit_bytes=58 * 1024 * 1024
+            collective_id=0, has_side_effects=True, vmem_limit_bytes=54 * 1024 * 1024
         ),
     )(spectra, mic_pos, focus_pts, wavenumber)
     return csm, beam.reshape(all_focus // 8)

time: 78.4 us -> 74.2 us (0.946)
  local copies, waits for them, and re-layouts: 5.21 us -> 2.53 us
  Pallas kernels: 71.6 us -> 70.1 us
    unnamed x4, local copies, waits for them, and re-layouts: 5.21 us -> 2.53 us
    pallas_call x1, Pallas kernels: 71.6 us -> 70.1 us  [exchange(): pl.pallas_call(kernel, out_shape=(pltpu.VMEM((2, rows, all_mics), f32), j...]
where the time goes in v2:
time: 74.2 us; the launch traced here: 73.9 us
  Pallas kernels  70.1 us (94%)
  local copies, waits for them, and re-layouts  2.53 us (3%)
  between operations  1.29 us (2%)
    pallas_call x1, Pallas kernels, exchange(): pl.pallas_call(kernel, out_shape=(pltpu.VMEM((2, rows, all_mics), f32), j...  70.1 us
    unnamed x4, local copies, waits for them, and re-layouts  2.53 us

profile of v2, /device:TPU:0, one launch (start us, length us, event | category | flops | bytes accessed | tf_op | source)
XLA Modules:
  0.0 73.9 jit_solution(9573249757372710269)
XLA Ops:
  1.3 70.1 %shard_map.59 = (f32[2,256,2048]{2,1,0:T(8,128)S(1)}, f32[1,128]{1,0:T(1,128)}) custom-call(f32[2,256,1024]{2,1,0:T(8,128)} %x_ref.1, f32[3,2048]{1,0:T(4,128)} %mic_ref.1, f32[3,1024]{1,0:T(4,128)} %foc_ref.1, f32[1]{0:T(128)S(6)} %copy.9.wave_ref), custom_call_target="tpu_custom_call" | custom-call | tf_op jit(solution)/shard_map/pallas_call | solution.py:427
  71.4 0.0 copy-start
  71.4 2.0 %copy.8 = f32[2,256,2048]{2,1,0:T(8,128)} copy(f32[2,256,2048]{2,1,0:T(8,128)S(1)} %get-tuple-element.6) | data formatting | bytes 8388608
  73.4 0.0 copy-done
  73.4 0.5 copy.10
Async XLA Ops:
  71.4 2.0 %copy-start = (f32[1,128]{1,0:T(1,128)S(1)}, f32[1,128]{1,0:T(1,128)}, u32[]{:S(2)}) copy-start(f32[1,128]{1,0:T(1,128)} %get-tuple-element.5) | copy-start | bytes 1540

commit v3 on v2

--- a/solution.py
+++ b/solution.py
@@ -184,8 +184,7 @@
     for t in range(2):
         main_copy(t, 0).start()
         main_copy(t, 1).start()
-        if t == 0:
-            sib_copy.start()
+    sib_copy.start()
     own_copy = pltpu.make_async_copy(x_ref, own, loc_sem)
     own_copy.start()
 

time: 74.2 us -> 74.2 us (level)
  no operation moved by 1% of the time
where the time goes in v3:
time: 74.2 us; the launch traced here: 73.9 us
  Pallas kernels  70.1 us (94%)
  local copies, waits for them, and re-layouts  2.53 us (3%)
  between operations  1.29 us (2%)
    pallas_call x1, Pallas kernels, exchange(): pl.pallas_call(kernel, out_shape=(pltpu.VMEM((2, rows, all_mics), f32), j...  70.1 us
    unnamed x4, local copies, waits for them, and re-layouts  2.53 us

profile of v3, /device:TPU:0, one launch (start us, length us, event | category | flops | bytes accessed | tf_op | source)
XLA Modules:
  0.0 73.9 jit_solution(17466026116524881367)
XLA Ops:
  1.3 70.1 %shard_map.59 = (f32[2,256,2048]{2,1,0:T(8,128)S(1)}, f32[1,128]{1,0:T(1,128)}) custom-call(f32[2,256,1024]{2,1,0:T(8,128)} %x_ref.1, f32[3,2048]{1,0:T(4,128)} %mic_ref.1, f32[3,1024]{1,0:T(4,128)} %foc_ref.1, f32[1]{0:T(128)S(6)} %copy.9.wave_ref), custom_call_target="tpu_custom_call" | custom-call | tf_op jit(solution)/shard_map/pallas_call | solution.py:426
  71.4 0.0 copy-start
  71.4 2.0 %copy.8 = f32[2,256,2048]{2,1,0:T(8,128)} copy(f32[2,256,2048]{2,1,0:T(8,128)S(1)} %get-tuple-element.6) | data formatting | bytes 8388608
  73.4 0.0 copy-done
  73.4 0.5 copy.10
Async XLA Ops:
  71.4 2.0 %copy-start = (f32[1,128]{1,0:T(1,128)S(1)}, f32[1,128]{1,0:T(1,128)}, u32[]{:S(2)}) copy-start(f32[1,128]{1,0:T(1,128)} %get-tuple-element.5) | copy-start | bytes 1540

commit v4 on v3

--- a/solution.py
+++ b/solution.py
@@ -257,10 +257,14 @@
 
         def tile(n, carry):
             lanes = pl.ds(pl.multiple_of(n * width, width), width)
-            c = [(chl[0, k, :m, :], chl[1, k, :m, :]) for k in range(2)]
-            g = [right(k, lanes) for k in range(2)]
-            zr = dot3(dot_nn, c[0], g[0]) - dot3(dot_nn, c[1], g[1])
-            zi = dot3(dot_nn, c[0], g[1]) + dot3(dot_nn, c[1], g[0])
+            sums = []
+            for k in range(2):
+                high, low = right(k, lanes)
+                a = dot_nn(chl[: 4 * m, :], high)
+                b = dot_nn(chl[: 2 * m, :], low)
+                sums.append([a[i * m : (i + 1) * m] + a[(2 + i) * m : (3 + i) * m] + b[i * m : (i + 1) * m] for i in range(2)])
+            zr = sums[0][0] - sums[1][1]
+            zi = sums[1][0] + sums[0][1]
             lr, li = left(0, lanes), left(1, lanes)
             p = lr * zr + li * zi
             p = jnp.sum(p.reshape(m // 8, 8, width), axis=0)
@@ -278,8 +282,8 @@
                 c = lax.broadcasted_iota(jnp.int32, (BLOCK, BLOCK), 1)
                 value = jnp.where((r == c) & drop_diagonal, 0.0, value)
             high, low = split(value)
-            chl[0, k, :m, :] = high
-            chl[1, k, :m, :] = low
+            chl[k * m : (k + 1) * m, :] = high
+            chl[(2 + k) * m : (3 + k) * m, :] = low
 
         def left(k, lanes):
             value = gh[0, k, row:, lanes].astype(jnp.float32) + gl[0, k, row:, lanes].astype(jnp.float32)
@@ -317,8 +321,8 @@
         for k in range(2):
             for b in range(2):
                 high, low = split(dbuf[2 * a + b, k])
-                chl[0, k, :HALF, b * HALF : (b + 1) * HALF] = high
-                chl[1, k, :HALF, b * HALF : (b + 1) * HALF] = low
+                chl[k * HALF : (k + 1) * HALF, b * HALF : (b + 1) * HALF] = high
+                chl[(2 + k) * HALF : (3 + k) * HALF, b * HALF : (b + 1) * HALF] = low
 
         def left(k, lanes):
             v = 2 + 2 * a
@@ -444,7 +448,7 @@
             pltpu.VMEM((6, 2, rows, all_focus), bf16),
             pltpu.VMEM((6, 2, rows, all_focus), bf16),
             pltpu.VMEM((6, 2, rows, rows), f32),
-            pltpu.VMEM((2, 2, rows, rows), bf16),
+            pltpu.VMEM((4 * rows, rows), bf16),
             pltpu.VMEM((4, 2, HALF, HALF), f32),
             pltpu.VMEM((4, 2, HALF, HALF), f32),
             pltpu.VMEM((8, all_focus), f32),

time: 74.2 us -> 74 us (level)
  no operation moved by 1% of the time
where the time goes in v4:
time: 74 us; the launch traced here: 73.8 us
  Pallas kernels  70 us (95%)
  local copies, waits for them, and re-layouts  2.53 us (3%)
  between operations  1.29 us (2%)
    pallas_call x1, Pallas kernels, exchange(): pl.pallas_call(kernel, out_shape=(pltpu.VMEM((2, rows, all_mics), f32), j...  70 us
    unnamed x4, local copies, waits for them, and re-layouts  2.53 us

profile of v4, /device:TPU:0, one launch (start us, length us, event | category | flops | bytes accessed | tf_op | source)
XLA Modules:
  0.0 73.8 jit_solution(12474720407780927901)
XLA Ops:
  1.3 70.0 %shard_map.59 = (f32[2,256,2048]{2,1,0:T(8,128)S(1)}, f32[1,128]{1,0:T(1,128)}) custom-call(f32[2,256,1024]{2,1,0:T(8,128)} %x_ref.1, f32[3,2048]{1,0:T(4,128)} %mic_ref.1, f32[3,1024]{1,0:T(4,128)} %foc_ref.1, f32[1]{0:T(128)S(6)} %copy.9.wave_ref), custom_call_target="tpu_custom_call" | custom-call | tf_op jit(solution)/shard_map/pallas_call | solution.py:430
  71.2 0.0 copy-start
  71.3 2.0 %copy.8 = f32[2,256,2048]{2,1,0:T(8,128)} copy(f32[2,256,2048]{2,1,0:T(8,128)S(1)} %get-tuple-element.6) | data formatting | bytes 8388608
  73.3 0.0 copy-done
  73.3 0.5 copy.10
Async XLA Ops:
  71.2 2.0 %copy-start = (f32[1,128]{1,0:T(1,128)S(1)}, f32[1,128]{1,0:T(1,128)}, u32[]{:S(2)}) copy-start(f32[1,128]{1,0:T(1,128)} %get-tuple-element.5) | copy-start | bytes 1540
